TPU v7x, 32 devices: a whole 2x2x4 slice. The times are simulated.
32 devices in a mesh: xi: 4 (over z), eta: 2 (over y), zeta: 4 (over x, core).
Axes of the slice: x: 2, y: 2, z: 4, core: 2. Of those that a mesh axis runs over, the one named last changes fastest.
Arguments:
- residual: float32 [5, 32, 32, 256], P(None, 'zeta', 'xi', 'eta'), may hold values from -6 to 6
- flow_state: float32 [5, 32, 32, 256], P(None, 'zeta', 'xi', 'eta'), may hold values from -6 to 6
- factors_zeta: float32 [3, 5, 32, 32, 256], P(None, None, 'zeta', 'xi', 'eta'), may hold values from -1.5 to 1.5, as said below
- factors_eta: float32 [3, 5, 32, 32, 256], P(None, None, 'zeta', 'xi', 'eta'), may hold values from -1.5 to 1.5, as said below
- factors_xi: float32 [3, 5, 32, 32, 256], P(None, None, 'zeta', 'xi', 'eta'), may hold values from -1.5 to 1.5, as said below
Outputs:
- update: float32 [5, 32, 32, 256], P(None, 'zeta', 'xi', 'eta')
Inputs may be any that keep to these rules, and one draw needn't show every extreme that they name: `factors_zeta`: F[g,2] is positive; the operator of each line is nonsingular. `factors_eta`: F[g,2] is positive; the operator of each line is nonsingular. `factors_xi`: F[g,2] is positive; the operator of each line is nonsingular.
All inputs are finite; a program needn't handle non-finite values.
Results may differ from a plain program's by a relative error of at most 0.000053.
Values sent between devices are 32-bit elements; how exact they have to be, the bound alone decides.
A program may use at most 128 MiB of HBM per device.

v0:
```python
import functools

import jax
import jax.numpy as jnp
from jax import lax
from jax.experimental import pallas as pl
from jax.experimental.pallas import tpu as pltpu
from jax.sharding import PartitionSpec as P

field_group = (0, 0, 0, 1, 2)
dissipation = 0.05
sublanes = 8
MESH = pl.DeviceIdType.MESH


def spread(planes):
    return jnp.concatenate([planes[g : g + 1] for g in field_group], 0)


def forward_sweep(steps, factor, value, recent, before):
    rows = []
    for s in range(steps):
        now = -(factor(0, s) * recent + factor(1, s) * before)
        if value is not None:
            now = now + value(s)
        rows.append(now)
        recent, before = now, recent
    return rows


def backward_sweep(steps, factor, value, recent, before, keep):
    rows = [None] * steps
    for s in reversed(range(steps)):
        now = factor(2, s) * value(s) - factor(3, s) * recent - factor(4, s) * before
        rows[s] = now
        keep(s, now)
        recent, before = now, recent
    return rows


def responses(steps, factor, keep):
    one = jnp.ones_like(factor(0, 0))
    zero = jnp.zeros_like(one)
    lift = lambda k, s: factor(k, s)[None]
    forward = forward_sweep(
        steps, lift, None, jnp.stack([one, zero]), jnp.stack([zero, one])
    )
    none = jnp.zeros((2,) + one.shape, jnp.float32)
    backward = backward_sweep(
        steps,
        lift,
        lambda s: jnp.concatenate([forward[s], none], 0),
        jnp.stack([zero, zero, one, zero]),
        jnp.stack([zero, zero, zero, one]),
        keep,
    )
    return jnp.concatenate([forward[-1], forward[-2], backward[0], backward[1]], 0)


def chain(count, matrices, offsets, into, closed):
    c1, c2, d1, d2 = into
    entered = []
    for q in range(count):
        entered.append((c1, c2))
        if q < count - 1 or not closed:
            m, o = matrices(q), offsets(q)
            n1, n2 = m[0] * c1 + m[1] * c2, m[2] * c1 + m[3] * c2
            c1, c2 = (n1, n2) if o is None else (o[0] + n1, o[1] + n2)
    out = (c1, c2)
    result = [None] * count
    for q in reversed(range(count)):
        c1, c2 = entered[q]
        result[q] = (c1, c2, d1, d2)
        if q > 0 or not closed:
            m, o = matrices(q), offsets(q)
            n1, n2 = m[4] * c1 + m[5] * c2, m[8] * c1 + m[9] * c2
            if o is not None:
                n1, n2 = o[2] + n1, o[3] + n2
            d1, d2 = n1 + (m[6] * d1 + m[7] * d2), n2 + (m[10] * d1 + m[11] * d2)
    return result, out + (d1, d2)


class Exchange:
    def __init__(self, axis, count, send_sem, recv_sem):
        self.axis, self.count = axis, count
        self.send_sem, self.recv_sem = send_sem, recv_sem
        self.me = lax.axis_index(axis)

    def peers(self):
        return [lax.rem(self.me + k, self.count) for k in range(1, self.count)]

    def copy(self, kind, source, slots, p, slot, cut):
        pick = (lambda ref: ref) if cut is None else (lambda ref: ref.at[cut[0] : cut[1]])
        return pltpu.make_async_remote_copy(
            src_ref=pick(source(p)),
            dst_ref=pick(slots.at[slot]),
            send_sem=self.send_sem.at[kind, p],
            recv_sem=self.recv_sem.at[kind, slot],
            device_id={self.axis: p},
            device_id_type=MESH,
        )

    def start(self, kind, source, slots, cut=None, sends=None):
        for p in self.peers():
            go = lambda p=p: self.copy(kind, source, slots, p, self.me, cut).start()
            go() if sends is None else pl.when(sends(self.me, p))(go)

    def wait_recv(self, kind, source, slots, cut=None, sends=None):
        for p in self.peers():
            go = lambda p=p: self.copy(kind, source, slots, p, p, cut).wait_recv()
            go() if sends is None else pl.when(sends(p, self.me))(go)

    def wait_send(self, kind, source, slots, cut=None, sends=None):
        for p in self.peers():
            go = lambda p=p: self.copy(kind, source, slots, p, self.me, cut).wait_send()
            go() if sends is None else pl.when(sends(self.me, p))(go)


class Split:
    def __init__(self, exchange, m_send, m_slots, o_send, o_slots, r_send, r_slots, full):
        self.x = exchange
        self.m_send, self.m_slots = m_send, m_slots
        self.o_send, self.o_slots = o_send, o_slots
        self.r_send, self.r_slots, self.full = r_send, r_slots, full
        self.parts = m_send.shape[0]
        self.rows = sublanes // self.parts
        pick = (lambda p: p) if self.parts > 1 else (lambda p: 0)
        last = exchange.count - 1
        m_from = lambda p: m_send.at[pick(p)]
        o_from = lambda p: o_send.at[pick(p)]
        r_from = lambda p: r_send.at[p]
        self.matrices = (0, m_from, m_slots)
        self.ahead = (1, o_from, o_slots, (0, 2), lambda a, b: a < last)
        self.behind = (2, o_from, o_slots, (2, 4), lambda a, b: a > 0)
        self.carried = (3, r_from, r_slots, (0, 2), lambda a, b: b > 0)
        self.returned = (4, r_from, r_slots, (2, 4), lambda a, b: b < last)
        self.pick = pick

    def clear_ends(self):
        if self.parts > 1:
            nothing = jnp.zeros((self.parts, 2) + self.r_slots.shape[2:], jnp.float32)

            @pl.when(self.x.me == 0)
            def _():
                self.r_slots[:, 0:2] = nothing

            @pl.when(self.x.me == self.x.count - 1)
            def _():
                self.r_slots[:, 2:4] = nothing

    def put(self, route, value, send, slots, lo):
        hi = lo + value.shape[0]
        for p in range(self.parts):
            send[p, lo:hi] = value[:, :, p * self.rows : (p + 1) * self.rows, :]
        slots[self.x.me, lo:hi] = send[self.pick(self.x.me), lo:hi]
        self.x.start(*route)

    def put_matrices(self, value):
        self.put(self.matrices, value, self.m_send, self.m_slots, 0)

    def put_ahead(self, value):
        self.put(self.ahead, value, self.o_send, self.o_slots, 0)

    def put_behind(self, value):
        self.put(self.behind, value, self.o_send, self.o_slots, 2)

    def solve(self):
        x = self.x
        for route in (self.matrices, self.ahead, self.behind):
            x.wait_recv(*route)
        zero = jnp.zeros(self.o_slots.shape[2:], jnp.float32)
        solved, _ = chain(
            x.count,
            lambda q: [spread(self.m_slots[q, k]) for k in range(12)],
            lambda q: [self.o_slots[q, k] for k in range(4)],
            (zero,) * 4,
            True,
        )
        for q, planes in enumerate(solved):
            for k in range(4):
                self.r_send[q, k] = planes[k]
        if self.parts > 1:
            x.start(*self.carried)
            x.start(*self.returned)
            me = x.me

            @pl.when(me > 0)
            def _():
                self.r_slots[me, 0:2] = self.r_send[me, 0:2]

            @pl.when(me < x.count - 1)
            def _():
                self.r_slots[me, 2:4] = self.r_send[me, 2:4]

    def result(self):
        x = self.x
        if self.parts == 1:
            return [self.r_send[x.me, k] for k in range(4)]
        x.wait_recv(*self.carried)
        x.wait_recv(*self.returned)
        for p in range(self.parts):
            self.full[:, :, p * self.rows : (p + 1) * self.rows, :] = self.r_slots[p]
        return [self.full[k] for k in range(4)]

    def finish(self):
        for route in (self.matrices, self.ahead, self.behind):
            self.x.wait_send(*route)
        if self.parts > 1:
            self.x.wait_send(*self.carried)
            self.x.wait_send(*self.returned)


def corrected(local, response, incoming, lift):
    total = local
    for k in range(4):
        total = total + lift(response[k]) * incoming[k]
    return total


def kernel(
    counts, residual_hbm, flow_hbm, f_zeta_hbm, f_eta_hbm, f_xi_hbm, out,
    residual, flow, f_zeta, f_eta, f_xi, in_sem,
    z_msend, z_mslots, z_osend, z_oslots, z_rsend, z_rslots, z_full, z_ss, z_rs,
    x_msend, x_mslots, x_osend, x_oslots, x_rsend, x_rslots, x_full, x_ss, x_rs,
    e_matrices, e_msend, e_mslots, e_offsets, e_osend, e_oslots, e_result, e_own, e_inner,
    e_ss, e_rs,
    z_response, x_response, e_response, lines, turned, turned_factors,
    hz, hx_send, hx, he_send, he, padded, source, h_ss, h_rs,
):
    n_xi, n_eta, n_zeta = counts
    fields, cz, cx, cy = flow.shape
    planes = fields * cz
    xz = Exchange("zeta", n_zeta, z_ss, z_rs)
    xe = Exchange("eta", n_eta, e_ss, e_rs)
    xx = Exchange("xi", n_xi, x_ss, x_rs)
    zeta = Split(xz, z_msend, z_mslots, z_osend, z_oslots, z_rsend, z_rslots, z_full)
    xi = Split(xx, x_msend, x_mslots, x_osend, x_oslots, x_rsend, x_rslots, x_full)

    barrier = pltpu.get_barrier_semaphore()
    greeted = 0
    for x in (xz, xe, xx):
        for p in x.peers():
            pl.semaphore_signal(barrier, inc=1, device_id={x.axis: p}, device_id_type=MESH)
            greeted += 1

    loads = [
        pltpu.make_async_copy(src, dst, in_sem.at[k])
        for k, (src, dst) in enumerate(
            (
                (flow_hbm, flow),
                (f_zeta_hbm, f_zeta),
                (f_xi_hbm, f_xi),
                (residual_hbm, residual),
                (f_eta_hbm, f_eta),
            )
        )
    ]
    for load in loads:
        load.start()
    zeta.clear_ends()
    xi.clear_ends()
    loads[0].wait()

    per_pack = cy // 4
    lane = lax.broadcasted_iota(jnp.int32, (cx, cy), 1)
    packs = [jnp.zeros((cx, cy), jnp.float32) for _ in range(he_send.shape[0])]
    eta_part = []
    for k in range(planes):
        at = k % per_pack
        v = flow[k // cz, k % cz]
        up1, up2 = pltpu.roll(v, 1, 1), pltpu.roll(v, 2, 1)
        down1, down2 = pltpu.roll(v, cy - 1, 1), pltpu.roll(v, cy - 2, 1)
        near_low, near_high = lane < 1, lane >= cy - 1
        far_low, far_high = lane < 2, lane >= cy - 2
        near = jnp.where(near_low, 0.0, up1) + jnp.where(near_high, 0.0, down1)
        far = jnp.where(far_low, 0.0, up2) + jnp.where(far_high, 0.0, down2)
        eta_part.append(far - 4.0 * near)
        near = jnp.where(near_low, up1, jnp.where(near_high, down1, 0.0))
        far = jnp.where(far_low, up2, jnp.where(far_high, down2, 0.0))
        face = -dissipation * (far - 4.0 * near)
        moved = pltpu.roll(face, (4 * at + 2) % cy, 1)
        packs[k // per_pack] = jnp.where(lane // 4 == at, moved, packs[k // per_pack])
    for k, pack in enumerate(packs):
        he_send[k] = pack
    row = lambda x: flow[:, :, x : x + 1, :]
    hx_send[0, :, :, 0:1, :] = -dissipation * (row(cx - 2) - 4.0 * row(cx - 1))
    hx_send[0, :, :, 1:2, :] = -dissipation * row(cx - 1)
    hx_send[1, :, :, 0:1, :] = -dissipation * row(0)
    hx_send[1, :, :, 1:2, :] = -dissipation * (row(1) - 4.0 * row(0))

    pl.semaphore_wait(barrier, greeted)

    halos = (
        (xx, hx, lambda side: hx_send.at[side]),
        (xe, he, lambda side: he_send),
        (xz, hz, lambda side: flow.at[:, cz - 2 : cz] if side == 0 else flow.at[:, 0:2]),
    )

    def halo_copy(number, side):
        x, slots, origin = halos[number]
        step = 1 if side == 0 else x.count - 1
        return pltpu.make_async_remote_copy(
            src_ref=origin(side),
            dst_ref=slots.at[side],
            send_sem=h_ss.at[number, side],
            recv_sem=h_rs.at[number, side],
            device_id={x.axis: lax.rem(x.me + step, x.count)},
            device_id_type=MESH,
        )

    for number, (x, slots, origin) in enumerate(halos):
        for side in range(2):
            sends = x.me < x.count - 1 if side == 0 else x.me > 0
            has = x.me > 0 if side == 0 else x.me < x.count - 1
            pl.when(sends)(lambda number=number, side=side: halo_copy(number, side).start())

            @pl.when(jnp.logical_not(has))
            def _(slots=slots, side=side):
                slots[side] = jnp.zeros(slots.shape[1:], jnp.float32)

    loads[1].wait()

    def keep_z(s, now):
        z_response[s] = now

    zeta.put_matrices(responses(cz, lambda k, s: f_zeta[:, k, s], keep_z))

    state = flow[...]
    nothing = jnp.zeros((fields, cz, 2, cy), jnp.float32)
    padded[:, :, 8 - 2 : 8, :] = nothing
    padded[:, :, 8 : 8 + cx, :] = state
    padded[:, :, 8 + cx : 8 + cx + 2, :] = nothing
    none = jnp.zeros((fields, 2, cx, cy), jnp.float32)
    long = jnp.concatenate([none, state, none], 1)
    near = (padded[:, :, 7 : 7 + cx, :] + padded[:, :, 9 : 9 + cx, :]) + (
        long[:, 1 : 1 + cz] + long[:, 3 : 3 + cz]
    )
    far = (padded[:, :, 6 : 6 + cx, :] + padded[:, :, 10 : 10 + cx, :]) + (
        long[:, 0:cz] + long[:, 4 : 4 + cz]
    )
    total_part = 18.0 * state - 4.0 * near + far + jnp.stack(eta_part).reshape(flow.shape)
    loads[3].wait()
    source[...] = residual[...] - dissipation * total_part

    loads[2].wait()

    def xi_factor(k, s):
        return jnp.stack(
            [f_xi[pl.ds((g * 5 + k) * cz * cx + s, cz, stride=cx), :] for g in range(3)]
        )

    def keep_x(s, now):
        x_response[s] = now

    xi.put_matrices(responses(cx, xi_factor, keep_x))

    for number, (x, slots, origin) in enumerate(halos):
        for side in range(2):
            has = x.me > 0 if side == 0 else x.me < x.count - 1
            pl.when(has)(lambda number=number, side=side: halo_copy(number, side).wait_recv())

    source[:, :, 0:2, :] += hx[0]
    source[:, :, cx - 2 : cx, :] += hx[1]
    zeta_faces = {
        0: hz[0, :, 0] - 4.0 * hz[0, :, 1],
        1: hz[0, :, 1],
        cz - 2: hz[1, :, 0],
        cz - 1: hz[1, :, 1] - 4.0 * hz[1, :, 0],
    }
    faces = [jnp.where(lane % 4 >= 2, he[0, k], he[1, k]) for k in range(he.shape[1])]
    edge = jnp.logical_or(lane < 2, lane >= cy - 2)

    def eta_face(f, z):
        k = f * cz + z
        back = (cy - (4 * (k % per_pack) + 2)) % cy
        return jnp.where(edge, pltpu.roll(faces[k // per_pack], back, 1), 0.0)

    def source_plane(z):
        value = source[:, z] + jnp.stack([eta_face(f, z) for f in range(fields)])
        if z in zeta_faces:
            value = value - dissipation * zeta_faces[z]
        return value

    z_factor = lambda k, s: spread(f_zeta[:, k, s])
    zero = jnp.zeros((fields, cx, cy), jnp.float32)
    forward = forward_sweep(cz, z_factor, source_plane, zero, zero)
    zeta.put_ahead(jnp.stack([forward[-1], forward[-2]]))
    local = backward_sweep(cz, z_factor, lambda s: forward[s], zero, zero, lambda s, now: None)
    zeta.put_behind(jnp.stack([local[0], local[1]]))

    loads[4].wait()
    tiles = lines.shape[0] // cy
    steps = cy // sublanes
    total = lines.shape[0]
    order = list(field_group) + [field_group[-1]] * (total // (cz * cx) - fields)
    for k in range(5):
        whole = jnp.concatenate([f_eta[g * 5 + k] for g in order], 0)
        for t in range(tiles):
            turned_factors[k * total + t * cy : k * total + (t + 1) * cy, :] = whole[
                t * cy : (t + 1) * cy
            ].T

    zeta.solve()

    def eta_factor(k, s):
        return turned_factors[
            pl.ds(k * total + s, tiles * sublanes, stride=steps), :
        ].reshape(tiles, sublanes, cy)

    def keep_e(s, now):
        e_response[s] = now

    e_matrices[...] = responses(steps, eta_factor, keep_e)
    chunk = lambda c: [e_matrices[k, :, c : c + 1, :] for k in range(12)]
    one, zero = jnp.ones((1, tiles, 1, cy), jnp.float32), jnp.zeros((1, tiles, 1, cy), jnp.float32)
    unit = lambda j: jnp.concatenate([one if i == j else zero for i in range(4)], 0)
    inner, left = chain(sublanes, chunk, lambda c: None, [unit(j) for j in range(4)], False)
    for c, values in enumerate(inner):
        for k in range(4):
            e_inner[k, :, :, c : c + 1, :] = values[k]
    e_msend[...] = jnp.concatenate([left[0][0:2], left[1][0:2], left[2], left[3]], 0)
    e_mslots[xe.me] = e_msend[...]
    xe.start(0, lambda p: e_msend, e_mslots)

    incoming = zeta.result()
    for s in range(cz):
        done = corrected(local[s], z_response[s], incoming, spread)
        for f in range(fields):
            lines[(f * cz + s) * cx : (f * cz + s + 1) * cx, :] = done[f]
    if total > planes * cx:
        lines[planes * cx : total, :] = jnp.zeros((total - planes * cx, cy), jnp.float32)

    for t in range(tiles):
        turned[t * cy : (t + 1) * cy, :] = lines[t * cy : (t + 1) * cy, :].T
    zero = jnp.zeros((tiles, sublanes, cy), jnp.float32)

    def at_step(s):
        return pl.ds(s, tiles * sublanes, stride=steps)

    forward = forward_sweep(
        steps, eta_factor, lambda s: turned[at_step(s), :].reshape(zero.shape), zero, zero
    )
    local = backward_sweep(
        steps, eta_factor, lambda s: forward[s], zero, zero, lambda s, now: None
    )
    for k, value in enumerate((forward[-1], forward[-2], local[0], local[1])):
        e_offsets[k] = value
    none = jnp.zeros((tiles, 1, cy), jnp.float32)
    inner, left = chain(
        sublanes,
        chunk,
        lambda c: [e_offsets[k, :, c : c + 1, :] for k in range(4)],
        (none,) * 4,
        False,
    )
    for k in range(4):
        e_osend[k] = left[k]
    e_oslots[xe.me] = e_osend[...]
    xe.start(1, lambda p: e_osend, e_oslots)
    for c, values in enumerate(inner):
        for k in range(4):
            e_own[k, :, c : c + 1, :] = values[k]
    xe.wait_recv(0, lambda p: e_msend, e_mslots)
    xe.wait_recv(1, lambda p: e_osend, e_oslots)
    solved, _ = chain(
        n_eta,
        lambda q: [e_mslots[q, k] for k in range(12)],
        lambda q: [e_oslots[q, k] for k in range(4)],
        (none,) * 4,
        True,
    )
    for q, values in enumerate(solved):
        for k in range(4):
            e_result[q, k] = values[k]
    enters = [e_result[xe.me, k] for k in range(4)]
    incoming = []
    for k in range(4):
        value = e_own[k]
        for j in range(2 if k < 2 else 4):
            value = value + e_inner[k, j] * enters[j]
        incoming.append(value)
    for s in range(steps):
        done = corrected(local[s], e_response[s], incoming, lambda r: r)
        turned[at_step(s), :] = done.reshape(tiles * sublanes, cy)
    for t in range(tiles):
        lines[t * cy : (t + 1) * cy, :] = turned[t * cy : (t + 1) * cy, :].T

    x_factor = lambda k, s: spread(xi_factor(k, s))
    zero = jnp.zeros((fields, cz, cy), jnp.float32)
    forward = forward_sweep(
        cx,
        x_factor,
        lambda s: lines[pl.ds(s, planes, stride=cx), :].reshape(zero.shape),
        zero,
        zero,
    )
    xi.put_ahead(jnp.stack([forward[-1], forward[-2]]))
    local = backward_sweep(cx, x_factor, lambda s: forward[s], zero, zero, lambda s, now: None)
    xi.put_behind(jnp.stack([local[0], local[1]]))
    xi.solve()
    incoming = xi.result()
    for s in range(cx):
        done = corrected(local[s], x_response[s], incoming, spread)
        out[pl.ds(s, planes, stride=cx), :] = done.reshape(planes, cy)

    zeta.finish()
    xi.finish()
    xe.wait_send(0, lambda p: e_msend, e_mslots)
    xe.wait_send(1, lambda p: e_osend, e_oslots)
    for number, (x, slots, origin) in enumerate(halos):
        for side in range(2):
            sends = x.me < x.count - 1 if side == 0 else x.me > 0
            pl.when(sends)(lambda number=number, side=side: halo_copy(number, side).wait_send())


def split_scratch(count, fields, lanes):
    vmem = lambda *shape: pltpu.VMEM(shape, jnp.float32)
    parts = count if sublanes % count == 0 else 1
    rows = sublanes // parts
    return [
        vmem(parts, 12, 3, rows, lanes),
        vmem(count, 12, 3, rows, lanes),
        vmem(parts, 4, fields, rows, lanes),
        vmem(count, 4, fields, rows, lanes),
        vmem(count, 4, fields, rows, lanes),
        vmem(count, 4, fields, rows, lanes),
        vmem(4, fields, sublanes, lanes),
        pltpu.SemaphoreType.DMA((5, count)),
        pltpu.SemaphoreType.DMA((5, count)),
    ]


def on_device(counts, residual, flow_state, factors_zeta, factors_eta, factors_xi):
    n_xi, n_eta, n_zeta = counts
    fields, cz, cx, cy = flow_state.shape
    total = -(-(fields * cz * cx) // cy) * cy
    tiles = total // cy
    steps = cy // sublanes
    packs = -(-(fields * cz) // (cy // 4))
    vmem = lambda *shape: pltpu.VMEM(shape, jnp.float32)
    dma = pltpu.SemaphoreType.DMA
    whole = pl.BlockSpec(memory_space=pltpu.VMEM)
    scratch = (
        [
            vmem(fields, cz, cx, cy),
            vmem(fields, cz, cx, cy),
            vmem(3, 5, cz, cx, cy),
            vmem(15, cz * cx, cy),
            vmem(15 * cz * cx, cy),
            dma((5,)),
        ]
        + split_scratch(n_zeta, fields, cy)
        + split_scratch(n_xi, fields, cy)
        + [
            vmem(12, tiles, sublanes, cy),
            vmem(12, tiles, 1, cy),
            vmem(n_eta, 12, tiles, 1, cy),
            vmem(4, tiles, sublanes, cy),
            vmem(4, tiles, 1, cy),
            vmem(n_eta, 4, tiles, 1, cy),
            vmem(n_eta, 4, tiles, 1, cy),
            vmem(4, tiles, sublanes, cy),
            vmem(4, 4, tiles, sublanes, cy),
            dma((2, n_eta)),
            dma((2, n_eta)),
            vmem(cz, 4, 3, cx, cy),
            vmem(cx, 4, 3, cz, cy),
            vmem(steps, 4, tiles, sublanes, cy),
            vmem(total, cy),
            vmem(total, cy),
            vmem(5 * total, cy),
            vmem(2, fields, 2, cx, cy),
            vmem(2, fields, cz, 2, cy),
            vmem(2, fields, cz, 2, cy),
            vmem(packs, cx, cy),
            vmem(2, packs, cx, cy),
            vmem(fields, cz, cx + 16, cy),
            vmem(fields, cz, cx, cy),
            dma((3, 2)),
            dma((3, 2)),
        ]
    )
    update = pl.pallas_call(
        functools.partial(kernel, counts),
        out_shape=jax.ShapeDtypeStruct((fields * cz * cx, cy), jnp.float32),
        in_specs=[pl.BlockSpec(memory_space=pl.ANY)] * 5,
        out_specs=whole,
        scratch_shapes=scratch,
        compiler_params=pltpu.CompilerParams(
            collective_id=0, has_side_effects=True, vmem_limit_bytes=56 * 2**20
        ),
    )(
        residual,
        flow_state,
        factors_zeta,
        factors_eta.reshape(15, cz * cx, cy),
        factors_xi.reshape(15 * cz * cx, cy),
    )
    return update.reshape(flow_state.shape)


def solution(mesh):
    fields = P(None, "zeta", "xi", "eta")
    factors = P(None, None, "zeta", "xi", "eta")
    counts = tuple(mesh.shape[axis] for axis in ("xi", "eta", "zeta"))
    return jax.shard_map(
        functools.partial(on_device, counts),
        mesh=mesh,
        in_specs=(fields, fields, factors, factors, factors),
        out_specs=fields,
        check_vma=False,
    )
```

profile of v0, /device:TPU:0, one launch (start us, length us, event | category | flops | bytes accessed | tf_op | source)
XLA Modules:
  0.0 29.0 jit_solution(13054271830623535925)
XLA Ops:
  0.0 27.4 %shard_map.55 = f32[320,128]{1,0:T(8,128)} custom-call(f32[5,8,8,128]{3,2,1,0:T(8,128)} %residual_hbm.1, f32[5,8,8,128]{3,2,1,0:T(8,128)} %flow_hbm.1, f32[3,5,8,8,128]{4,3,2,1,0:T(8,128)} %f_zeta_hbm.1, f32[15,64,128]{2,1,0:T(8,128)} %bitcast.4, f32[960,128]{1,0:T(8,128)} %bitcast.5), custom_call_target="tpu_custom_call" | custom-call | tf_op jit(solution)/shard_map/pallas_call | solution.py:583
  27.4 1.6 %copy.7 = f32[5,8,8,128]{3,2,1,0:T(8,128)} copy(f32[5,8,8,128]{3,2,1,0:T(8,128)} %bitcast.3) | data formatting | bytes 327680
where the time goes:
time: 29.1 us; the launch traced here: 29 us
  Pallas kernels  27.4 us (94%)
  local copies, waits for them, and re-layouts  1.59 us (5%)
    pallas_call x1, Pallas kernels, on_device(): pl.pallas_call(functools.partial(kernel, counts), out_shape=jax.ShapeDtyp...  27.4 us
    unnamed x1, local copies, waits for them, and re-layouts  1.59 us

commit v1 on v0

--- a/solution.py
+++ b/solution.py
@@ -13,16 +13,36 @@
 MESH = pl.DeviceIdType.MESH
 
 
+line_order = (0, 3, 1, 4, 2)
+
+
 def spread(planes):
     return jnp.concatenate([planes[g : g + 1] for g in field_group], 0)
+
+
+def line_spread(planes):
+    return jnp.concatenate([planes[field_group[f]][None] for f in line_order], 0)
+
+
+def line_tiles(per_tile):
+    distinct, uses = [], []
+    for start in range(0, len(line_order), per_tile):
+        groups = [field_group[f] for f in line_order[start : start + per_tile]]
+        for number, have in enumerate(distinct):
+            if have[: len(groups)] == groups:
+                break
+        else:
+            number = len(distinct)
+            distinct.append(groups + [groups[-1]] * (per_tile - len(groups)))
+        uses.append(number)
+    return distinct, uses
 
 
 def forward_sweep(steps, factor, value, recent, before):
     rows = []
     for s in range(steps):
-        now = -(factor(0, s) * recent + factor(1, s) * before)
-        if value is not None:
-            now = now + value(s)
+        now = -(factor(1, s) * before) if value is None else value(s) - factor(1, s) * before
+        now = now - factor(0, s) * recent
         rows.append(now)
         recent, before = now, recent
     return rows
@@ -31,7 +51,7 @@
 def backward_sweep(steps, factor, value, recent, before, keep):
     rows = [None] * steps
     for s in reversed(range(steps)):
-        now = factor(2, s) * value(s) - factor(3, s) * recent - factor(4, s) * before
+        now = factor(2, s) * value(s) - factor(4, s) * before - factor(3, s) * recent
         rows[s] = now
         keep(s, now)
         recent, before = now, recent
@@ -117,8 +137,8 @@
 
 
 class Split:
-    def __init__(self, exchange, m_send, m_slots, o_send, o_slots, r_send, r_slots, full):
-        self.x = exchange
+    def __init__(self, exchange, lift, m_send, m_slots, o_send, o_slots, r_send, r_slots, full):
+        self.x, self.lift = exchange, lift
         self.m_send, self.m_slots = m_send, m_slots
         self.o_send, self.o_slots = o_send, o_slots
         self.r_send, self.r_slots, self.full = r_send, r_slots, full
@@ -171,7 +191,7 @@
         zero = jnp.zeros(self.o_slots.shape[2:], jnp.float32)
         solved, _ = chain(
             x.count,
-            lambda q: [spread(self.m_slots[q, k]) for k in range(12)],
+            lambda q: [self.lift(self.m_slots[q, k]) for k in range(12)],
             lambda q: [self.o_slots[q, k] for k in range(4)],
             (zero,) * 4,
             True,
@@ -224,7 +244,7 @@
     x_msend, x_mslots, x_osend, x_oslots, x_rsend, x_rslots, x_full, x_ss, x_rs,
     e_matrices, e_msend, e_mslots, e_offsets, e_osend, e_oslots, e_result, e_own, e_inner,
     e_ss, e_rs,
-    z_response, x_response, e_response, lines, turned, turned_factors,
+    z_response, x_response, e_response, x_factors, e_factors, lines, turned, turned_factors,
     hz, hx_send, hx, he_send, he, padded, source, h_ss, h_rs,
 ):
     n_xi, n_eta, n_zeta = counts
@@ -233,8 +253,8 @@
     xz = Exchange("zeta", n_zeta, z_ss, z_rs)
     xe = Exchange("eta", n_eta, e_ss, e_rs)
     xx = Exchange("xi", n_xi, x_ss, x_rs)
-    zeta = Split(xz, z_msend, z_mslots, z_osend, z_oslots, z_rsend, z_rslots, z_full)
-    xi = Split(xx, x_msend, x_mslots, x_osend, x_oslots, x_rsend, x_rslots, x_full)
+    zeta = Split(xz, spread, z_msend, z_mslots, z_osend, z_oslots, z_rsend, z_rslots, z_full)
+    xi = Split(xx, line_spread, x_msend, x_mslots, x_osend, x_oslots, x_rsend, x_rslots, x_full)
 
     barrier = pltpu.get_barrier_semaphore()
     greeted = 0
@@ -344,10 +364,13 @@
 
     loads[2].wait()
 
+    for s in range(cx):
+        for k in range(5):
+            for g in range(3):
+                x_factors[k, s, g] = f_xi[pl.ds((g * 5 + k) * cz * cx + s, cz, stride=cx), :]
+
     def xi_factor(k, s):
-        return jnp.stack(
-            [f_xi[pl.ds((g * 5 + k) * cz * cx + s, cz, stride=cx), :] for g in range(3)]
-        )
+        return x_factors[k, s]
 
     def keep_x(s, now):
         x_response[s] = now
@@ -392,27 +415,31 @@
     tiles = lines.shape[0] // cy
     steps = cy // sublanes
     total = lines.shape[0]
-    order = list(field_group) + [field_group[-1]] * (total // (cz * cx) - fields)
+    distinct, uses = line_tiles(cy // (cz * cx))
     for k in range(5):
-        whole = jnp.concatenate([f_eta[g * 5 + k] for g in order], 0)
-        for t in range(tiles):
-            turned_factors[k * total + t * cy : k * total + (t + 1) * cy, :] = whole[
-                t * cy : (t + 1) * cy
-            ].T
+        for t, groups in enumerate(distinct):
+            whole = jnp.concatenate([f_eta[g * 5 + k] for g in groups], 0)
+            turned_factors[t * cy : (t + 1) * cy, :] = whole.T
+        for s in range(steps):
+            e_factors[k, s] = turned_factors[
+                pl.ds(s, len(distinct) * sublanes, stride=steps), :
+            ].reshape(len(distinct), sublanes, cy)
+
+    def tiled(planes):
+        return jnp.concatenate([planes[u : u + 1] for u in uses], 0)
 
     zeta.solve()
 
     def eta_factor(k, s):
-        return turned_factors[
-            pl.ds(k * total + s, tiles * sublanes, stride=steps), :
-        ].reshape(tiles, sublanes, cy)
+        return e_factors[k, s]
 
     def keep_e(s, now):
         e_response[s] = now
 
     e_matrices[...] = responses(steps, eta_factor, keep_e)
     chunk = lambda c: [e_matrices[k, :, c : c + 1, :] for k in range(12)]
-    one, zero = jnp.ones((1, tiles, 1, cy), jnp.float32), jnp.zeros((1, tiles, 1, cy), jnp.float32)
+    one = jnp.ones((1, len(distinct), 1, cy), jnp.float32)
+    zero = jnp.zeros_like(one)
     unit = lambda j: jnp.concatenate([one if i == j else zero for i in range(4)], 0)
     inner, left = chain(sublanes, chunk, lambda c: None, [unit(j) for j in range(4)], False)
     for c, values in enumerate(inner):
@@ -425,8 +452,8 @@
     incoming = zeta.result()
     for s in range(cz):
         done = corrected(local[s], z_response[s], incoming, spread)
-        for f in range(fields):
-            lines[(f * cz + s) * cx : (f * cz + s + 1) * cx, :] = done[f]
+        for place, f in enumerate(line_order):
+            lines[(place * cz + s) * cx : (place * cz + s + 1) * cx, :] = done[f]
     if total > planes * cx:
         lines[planes * cx : total, :] = jnp.zeros((total - planes * cx, cy), jnp.float32)
 
@@ -434,21 +461,23 @@
         turned[t * cy : (t + 1) * cy, :] = lines[t * cy : (t + 1) * cy, :].T
     zero = jnp.zeros((tiles, sublanes, cy), jnp.float32)
 
+    eta_tiles = lambda k, s: tiled(e_factors[k, s])
+
     def at_step(s):
         return pl.ds(s, tiles * sublanes, stride=steps)
 
     forward = forward_sweep(
-        steps, eta_factor, lambda s: turned[at_step(s), :].reshape(zero.shape), zero, zero
+        steps, eta_tiles, lambda s: turned[at_step(s), :].reshape(zero.shape), zero, zero
     )
     local = backward_sweep(
-        steps, eta_factor, lambda s: forward[s], zero, zero, lambda s, now: None
+        steps, eta_tiles, lambda s: forward[s], zero, zero, lambda s, now: None
     )
     for k, value in enumerate((forward[-1], forward[-2], local[0], local[1])):
         e_offsets[k] = value
     none = jnp.zeros((tiles, 1, cy), jnp.float32)
     inner, left = chain(
         sublanes,
-        chunk,
+        lambda c: [tiled(plane) for plane in chunk(c)],
         lambda c: [e_offsets[k, :, c : c + 1, :] for k in range(4)],
         (none,) * 4,
         False,
@@ -464,7 +493,7 @@
     xe.wait_recv(1, lambda p: e_osend, e_oslots)
     solved, _ = chain(
         n_eta,
-        lambda q: [e_mslots[q, k] for k in range(12)],
+        lambda q: [tiled(e_mslots[q, k]) for k in range(12)],
         lambda q: [e_oslots[q, k] for k in range(4)],
         (none,) * 4,
         True,
@@ -477,15 +506,15 @@
     for k in range(4):
         value = e_own[k]
         for j in range(2 if k < 2 else 4):
-            value = value + e_inner[k, j] * enters[j]
+            value = value + tiled(e_inner[k, j]) * enters[j]
         incoming.append(value)
     for s in range(steps):
-        done = corrected(local[s], e_response[s], incoming, lambda r: r)
+        done = corrected(local[s], e_response[s], incoming, tiled)
         turned[at_step(s), :] = done.reshape(tiles * sublanes, cy)
     for t in range(tiles):
         lines[t * cy : (t + 1) * cy, :] = turned[t * cy : (t + 1) * cy, :].T
 
-    x_factor = lambda k, s: spread(xi_factor(k, s))
+    x_factor = lambda k, s: line_spread(xi_factor(k, s))
     zero = jnp.zeros((fields, cz, cy), jnp.float32)
     forward = forward_sweep(
         cx,
@@ -500,8 +529,9 @@
     xi.solve()
     incoming = xi.result()
     for s in range(cx):
-        done = corrected(local[s], x_response[s], incoming, spread)
-        out[pl.ds(s, planes, stride=cx), :] = done.reshape(planes, cy)
+        done = corrected(local[s], x_response[s], incoming, line_spread)
+        for place, f in enumerate(line_order):
+            out[pl.ds(f * cz * cx + s, cz, stride=cx), :] = done[place]
 
     zeta.finish()
     xi.finish()
@@ -537,6 +567,7 @@
     tiles = total // cy
     steps = cy // sublanes
     packs = -(-(fields * cz) // (cy // 4))
+    distinct = len(line_tiles(cy // (cz * cx))[0])
     vmem = lambda *shape: pltpu.VMEM(shape, jnp.float32)
     dma = pltpu.SemaphoreType.DMA
     whole = pl.BlockSpec(memory_space=pltpu.VMEM)
@@ -552,23 +583,25 @@
         + split_scratch(n_zeta, fields, cy)
         + split_scratch(n_xi, fields, cy)
         + [
-            vmem(12, tiles, sublanes, cy),
-            vmem(12, tiles, 1, cy),
-            vmem(n_eta, 12, tiles, 1, cy),
+            vmem(12, distinct, sublanes, cy),
+            vmem(12, distinct, 1, cy),
+            vmem(n_eta, 12, distinct, 1, cy),
             vmem(4, tiles, sublanes, cy),
             vmem(4, tiles, 1, cy),
             vmem(n_eta, 4, tiles, 1, cy),
             vmem(n_eta, 4, tiles, 1, cy),
             vmem(4, tiles, sublanes, cy),
-            vmem(4, 4, tiles, sublanes, cy),
+            vmem(4, 4, distinct, sublanes, cy),
             dma((2, n_eta)),
             dma((2, n_eta)),
             vmem(cz, 4, 3, cx, cy),
             vmem(cx, 4, 3, cz, cy),
-            vmem(steps, 4, tiles, sublanes, cy),
+            vmem(steps, 4, distinct, sublanes, cy),
+            vmem(5, cx, 3, cz, cy),
+            vmem(5, steps, distinct, sublanes, cy),
             vmem(total, cy),
             vmem(total, cy),
-            vmem(5 * total, cy),
+            vmem(distinct * cy, cy),
             vmem(2, fields, 2, cx, cy),
             vmem(2, fields, cz, 2, cy),
             vmem(2, fields, cz, 2, cy),
@@ -583,18 +616,23 @@
     update = pl.pallas_call(
         functools.partial(kernel, counts),
         out_shape=jax.ShapeDtypeStruct((fields * cz * cx, cy), jnp.float32),
-        in_specs=[pl.BlockSpec(memory_space=pl.ANY)] * 5,
+        in_specs=[pl.BlockSpec(memory_space=pltpu.HBM)] * 5,
         out_specs=whole,
         scratch_shapes=scratch,
         compiler_params=pltpu.CompilerParams(
-            collective_id=0, has_side_effects=True, vmem_limit_bytes=56 * 2**20
+            collective_id=0, has_side_effects=True, vmem_limit_bytes=24 * 2**20
         ),
     )(
-        residual,
-        flow_state,
-        factors_zeta,
-        factors_eta.reshape(15, cz * cx, cy),
-        factors_xi.reshape(15 * cz * cx, cy),
+        *(
+            pltpu.with_memory_space_constraint(operand, pltpu.HBM)
+            for operand in (
+                residual,
+                flow_state,
+                factors_zeta,
+                factors_eta.reshape(15, cz * cx, cy),
+                factors_xi.reshape(15 * cz * cx, cy),
+            )
+        )
     )
     return update.reshape(flow_state.shape)
 

time: 29.1 us -> 27.2 us (0.935)
  Pallas kernels: 27.4 us -> 26.4 us
  local copies, waits for them, and re-layouts: 1.59 us -> 0.67 us
    pallas_call x1, Pallas kernels: 27.4 us -> 26.4 us  [on_device(): pl.pallas_call(functools.partial(kernel, counts), out_shape=jax.ShapeDtyp...]
    unnamed x1, local copies, waits for them, and re-layouts: 1.59 us -> 0.67 us
where the time goes in v1:
time: 27.2 us; the launch traced here: 27.1 us
  Pallas kernels  26.4 us (97%)
  local copies, waits for them, and re-layouts  0.67 us (2%)
    pallas_call x1, Pallas kernels, on_device(): pl.pallas_call(functools.partial(kernel, counts), out_shape=jax.ShapeDtyp...  26.4 us
    unnamed x1, local copies, waits for them, and re-layouts  0.67 us

profile of v1, /device:TPU:0, one launch (start us, length us, event | category | flops | bytes accessed | tf_op | source)
XLA Modules:
  0.0 27.1 jit_solution(6331180697397329521)
XLA Ops:
  0.0 26.4 %shard_map.55 = f32[320,128]{1,0:T(8,128)S(1)} custom-call(f32[5,8,8,128]{3,2,1,0:T(8,128)} %residual_hbm.1, f32[5,8,8,128]{3,2,1,0:T(8,128)} %flow_hbm.1, f32[3,5,8,8,128]{4,3,2,1,0:T(8,128)} %f_zeta_hbm.1, f32[15,64,128]{2,1,0:T(8,128)} %bitcast.4, f32[960,128]{1,0:T(8,128)} %bitcast.5), custom_call_target="tpu_custom_call" | custom-call | tf_op jit(solution)/shard_map/pallas_call | solution.py:616
  26.4 0.7 %copy.7 = f32[5,8,8,128]{3,2,1,0:T(8,128)} copy(f32[5,8,8,128]{3,2,1,0:T(8,128)S(1)} %bitcast.3) | data formatting | bytes 327680
